TPU v7x, 256 devices: a whole 4x4x8 slice. The times are simulated.
256 devices in a mesh: section: 2 (over core), seq: 128 (over z, y, x).
Axes of the slice: x: 4, y: 4, z: 8, core: 2. Of those that a mesh axis runs over, the one named last changes fastest.
Arguments:
- queries: bfloat16 [32768, 4096], P('seq', 'section'), may hold values from -50 to 50
- key_rows: bfloat16 [32768, 4096], P('seq', 'section'), may hold values from -6 to 6
- value_rows: bfloat16 [32768, 4096], P('seq', 'section'), may hold values from -6 to 6
- block_pattern: int32 [256, 8], P('seq'), may hold values from 0 to 1, as said below
- out_weight: bfloat16 [4096, 4096], P('section'), may hold values from -0.09375 to 0.09375
- hidden: bfloat16 [32768, 4096], P('seq', 'section'), may hold values from -3 to 3
- norm_gain: float32 [4096], P('section'), may hold values from 0.5 to 1.5
Outputs:
- stream_out: bfloat16 [32768, 4096], P('seq', 'section')
- normed: bfloat16 [32768, 4096], P('seq', 'section')
Inputs may be any that keep to these rules, and one draw needn't show every extreme that they name: `block_pattern`: column 0 is 1 in every row: every query block attends its own block.
All inputs are finite; a program needn't handle non-finite values.
Results may differ from a plain program's by a relative error of at most 0.008.
Values may be sent and summed in bfloat16 or wider, within the bound.
No kernel may reach another device: no remote copies, remote signals or barrier semaphores. Data moves between devices by JAX's collectives and lax.ppermute only.
A program may use at most 128 MiB of HBM per device.

v0:
```python
import math

import jax
import jax.numpy as jnp
from jax import lax
from jax.sharding import PartitionSpec as P

D = 4096
HEAD_DIM = 128
BLOCK = 128
WINDOW_BLOCKS = 8
BLK_DEV = 2


def from_behind(block, axis, distance):
    devices = range(lax.axis_size(axis))
    route = [(i - distance, i) for i in devices if i - distance in devices]
    return lax.ppermute(block, axis, route)


def window_mask(block_pattern, shard_index):
    key_blocks = WINDOW_BLOCKS - 1 + BLK_DEV
    query_block = jnp.arange(BLK_DEV, dtype=jnp.int32)[:, None]
    key_block = jnp.arange(key_blocks, dtype=jnp.int32)[None, :]
    offsets = query_block + (WINDOW_BLOCKS - 1) - key_block
    matches = offsets[:, :, None] == jnp.arange(WINDOW_BLOCKS, dtype=jnp.int32)[None, None, :]
    allowed = jnp.any(matches & (block_pattern[:, None, :] == 1), axis=2)
    global_key = shard_index * BLK_DEV - (WINDOW_BLOCKS - 1) + key_block
    allowed = allowed & (global_key >= 0)
    row_allowed = jnp.repeat(jnp.repeat(allowed, BLOCK, axis=0), BLOCK, axis=1)
    row_offsets = jnp.repeat(jnp.repeat(offsets, BLOCK, axis=0), BLOCK, axis=1)
    query_place = (jnp.arange(BLK_DEV * BLOCK, dtype=jnp.int32) % BLOCK)[:, None]
    key_place = (jnp.arange(key_blocks * BLOCK, dtype=jnp.int32) % BLOCK)[None, :]
    causal = (row_offsets > 0) | (key_place <= query_place)
    return row_allowed & causal


def attend(query_rows, key_all, value_all, visible):
    row_count = query_rows.shape[0]
    heads_here = query_rows.shape[1] // HEAD_DIM
    front_rows = (WINDOW_BLOCKS - 1) * BLOCK
    block_rows = math.gcd(row_count, 512)
    scaling = 1.0 / math.sqrt(HEAD_DIM)
    key_span = front_rows + block_rows
    query_group = query_rows.reshape(block_rows, heads_here, HEAD_DIM)
    key_group = key_all.reshape(key_span, heads_here, HEAD_DIM)
    value_group = value_all.reshape(key_span, heads_here, HEAD_DIM)
    scores = (
        jnp.einsum("qhd,khd->hqk", query_group, key_group, preferred_element_type=jnp.float32)
        * scaling
    )
    scores = jnp.where(visible[None], scores, -jnp.inf)
    largest = jnp.max(scores, axis=2, keepdims=True)
    exponent = jnp.exp(scores - largest)
    weights = (exponent / jnp.sum(exponent, axis=2, keepdims=True)).astype(jnp.bfloat16)
    mixture = jnp.einsum("hqk,khd->qhd", weights, value_group, preferred_element_type=jnp.float32)
    results = mixture.reshape(block_rows, heads_here * HEAD_DIM)
    return results.astype(jnp.bfloat16)


def shards(queries, key_rows, value_rows, block_pattern, out_weight, hidden, norm_gain):
    shard_index = lax.axis_index("seq")
    reach_count = (WINDOW_BLOCKS - 2) // BLK_DEV + 1
    tail_rows = (WINDOW_BLOCKS - 1 - (reach_count - 1) * BLK_DEV) * BLOCK
    received = []
    for offset in range(1, reach_count + 1):
        if offset == reach_count:
            outgoing = (
                key_rows[key_rows.shape[0] - tail_rows :],
                value_rows[value_rows.shape[0] - tail_rows :],
            )
        else:
            outgoing = (key_rows, value_rows)
        received.append(from_behind((outgoing[0], outgoing[1]), "seq", offset))
    ordered = received[::-1]
    key_all = jnp.concatenate([couple[0] for couple in ordered] + [key_rows], 0)
    value_all = jnp.concatenate([couple[1] for couple in ordered] + [value_rows], 0)
    visible = window_mask(block_pattern, shard_index)
    attended = attend(queries, key_all, value_all, visible)
    partial_value = jnp.dot(attended, out_weight, preferred_element_type=jnp.float32)
    projected = lax.psum_scatter(
        partial_value.astype(jnp.bfloat16), "section", scatter_dimension=1, tiled=True
    ).astype(jnp.float32)
    stream = hidden.astype(jnp.float32) + projected
    row_sums = lax.psum(jnp.sum(stream * stream, axis=1), "section")
    factor = lax.rsqrt(row_sums / D + 1e-06)
    normed = stream * factor[:, None] * norm_gain[None, :]
    return (stream.astype(jnp.bfloat16), normed.astype(jnp.bfloat16))


def solution(mesh):
    placed = (
        P("seq", "section"),
        P("seq", "section"),
        P("seq", "section"),
        P("seq", None),
        P("section", None),
        P("seq", "section"),
        P("section"),
    )
    return jax.shard_map(
        shards,
        mesh=mesh,
        in_specs=placed,
        out_specs=(P("seq", "section"), P("seq", "section")),
        check_vma=False,
    )
```

profile of v0, /device:TPU:1, one launch (start us, length us, event | category | flops | bytes accessed | tf_op | source)
XLA Modules:
  0.0 336.0 jit_solution(8462136048937641629)
XLA Ops:
  7.2 0.0 copy-start
  7.2 0.0 copy-start.4
  7.2 0.0 reduce-scatter.2.cloned.1.call-start
  7.2 1.6 copy.26
  8.9 4.9 %collective-permute-start.7 = (bf16[256,2048]{0,1:T(8,128)(2,1)S(1)}, bf16[256,2048]{0,1:T(8,128)(2,1)}, u32[]{:S(2)}, u32[]{:S(2)}) collective-permute-start(bf16[256,2048]{0,1:T(8,128)(2,1)S(1)} %copy.26), channel_id=1, source_target_pairs={{0,1},{1,2},{2,3},{3,4},{4,5},{5,6},{6,7},{7,8},{8,9},{9,10},{10,1... | collective-permute-start | bytes 3145736 | tf_op jit(solution)/shard_map/ppermute | solution.py:18
  13.8 4.5 %collective-permute-start.6 = (bf16[256,2048]{0,1:T(8,128)(2,1)S(1)}, bf16[256,2048]{0,1:T(8,128)(2,1)}, u32[]{:S(2)}, u32[]{:S(2)}) collective-permute-start(bf16[256,2048]{0,1:T(8,128)(2,1)S(1)} %copy.26), channel_id=1, source_target_pairs={{0,2},{1,3},{2,4},{3,5},{4,6},{5,7},{6,8},{7,9},{8,10},{9,11},{10,... | collective-permute-start | bytes 3145736 | tf_op jit(solution)/shard_map/ppermute | solution.py:18
  18.3 4.0 %collective-permute-start.5 = (bf16[256,2048]{0,1:T(8,128)(2,1)S(1)}, bf16[256,2048]{0,1:T(8,128)(2,1)}, u32[]{:S(2)}, u32[]{:S(2)}) collective-permute-start(bf16[256,2048]{0,1:T(8,128)(2,1)S(1)} %copy.26), channel_id=1, source_target_pairs={{0,3},{1,4},{2,5},{3,6},{4,7},{5,8},{6,9},{7,10},{8,11},{9,12},{10... | collective-permute-start | bytes 3145736 | tf_op jit(solution)/shard_map/ppermute | solution.py:18
  22.3 1.9 slice.6
  24.2 3.0 collective-permute-start
  27.1 0.8 slice.8
  28.0 2.9 collective-permute-start.4
  30.9 0.7 broadcast_compare_fusion.1
  31.6 0.1 broadcast_bitcast_fusion
  31.7 0.1 copy.24
  31.8 0.1 fusion.18
  31.9 0.1 copy.25
  32.0 0.1 broadcast_bitcast_fusion.1
  32.2 0.3 fusion.8
  32.5 72.9 %collective-permute-done.4 = bf16[128,2048]{0,1:T(8,128)(2,1)} collective-permute-done((bf16[128,2048]{0,1:T(8,128)(2,1)}, bf16[128,2048]{0,1:T(8,128)(2,1)}, u32[]{:S(2)}, u32[]{:S(2)}) %collective-permute-start.4) | collective-permute-done | bytes 524320 | tf_op jit(solution)/shard_map/ppermute | solution.py:18
  105.4 1.3 collective-permute-start.2
  106.7 1.1 constant_dynamic-update-slice_fusion.9
  107.9 0.0 collective-permute-done
  107.9 1.4 collective-permute-start.1
  109.3 1.9 constant_dynamic-update-slice_fusion.4
  111.1 0.0 collective-permute-done.5
  111.1 7.4 %collective-permute-start.3 = (bf16[256,2048]{1,0:T(8,128)(2,1)S(1)}, bf16[256,2048]{1,0:T(8,128)(2,1)}, u32[]{:S(2)}, u32[]{:S(2)}) collective-permute-start(bf16[256,2048]{1,0:T(8,128)(2,1)S(1)} %copy-done.4), channel_id=1, source_target_pairs={{0,1},{1,2},{2,3},{3,4},{4,5},{5,6},{6,7},{7,8},{8,9},{9,10},{10,1... | collective-permute-start | bytes 3145736 | tf_op jit(solution)/shard_map/ppermute | solution.py:18
  118.6 1.3 constant_dynamic-update-slice_fusion.8
  119.9 1.3 constant_dynamic-update-slice_fusion.7
  121.2 1.3 constant_dynamic-update-slice_fusion.6
  122.5 0.1 constant_dynamic-update-slice_fusion.5
  122.6 11.6 %collective-permute-done.1 = bf16[256,2048]{1,0:T(8,128)(2,1)S(1)} collective-permute-done((bf16[256,2048]{1,0:T(8,128)(2,1)S(1)}, bf16[256,2048]{1,0:T(8,128)(2,1)S(1)}, u32[]{:S(2)}, u32[]{:S(2)}) %collective-permute-start.1) | collective-permute-done | bytes 1048608 | tf_op jit(solution)/shard_map/ppermute | solution.py:18
  134.1 1.1 constant_dynamic-update-slice_fusion.3
  135.2 7.9 %convolution_multiply_fusion = f32[16,1152,256]{2,1,0:T(8,128)} fusion(bf16[1152,16,128]{0,2,1:T(8,128)(2,1)S(1)} %bitcast.55, bf16[256,2048]{1,0:T(8,128)(2,1)S(1)} %copy-done), kind=kOutput, calls=%fused_computation.2 | convolution fusion | flops 1212678144 | bytes 24641536 | tf_op jit(solution)/shard_map/qhd,khd->hqk/dot_general | solution.py:49
  143.2 1.1 constant_dynamic-update-slice_fusion.2
  144.2 8.2 %exponential_reduce_fusion = f32[16,256]{1,0:T(8,128)S(1)} fusion(pred[256,1152]{0,1:T(8,128)(4,1)S(1)} %fusion.8, bf16[1152,16,128]{0,2,1:T(8,128)(2,1)} %bitcast.56, bf16[256,2048]{1,0:T(8,128)(2,1)S(1)} %copy-done), kind=kOutput, calls=%fused_computation.6 | convolution fusion | flops 1226835072 | bytes 6078464 | tf_op jit(solution)/shard_map/sub | solution.py:54
  152.5 2.4 constant_dynamic-update-slice_fusion.1
  154.8 1.1 constant_dynamic-update-slice_fusion
  155.9 6.7 %copy.23 = bf16[1152,2048]{0,1:T(8,128)(2,1)} copy(bf16[1152,2048]{1,0:T(8,128)(2,1)} %constant_dynamic-update-slice_fusion) | data formatting | bytes 9437184 | tf_op jit(solution)/shard_map/concatenate | solution.py:77
  162.6 12.0 %fusion.7 = bf16[16,128,256]{2,1,0:T(8,128)(2,1)S(1)} fusion(bf16[1152,16,128]{0,2,1:T(8,128)(2,1)} %bitcast.57, f32[16,256]{1,0:T(8,128)S(1)} %exponential_reduce_fusion, f32[16,1152,256]{2,1,0:T(8,128)} %convolution_multiply_fusion, pred[256,1152]{0,1:T(8,128)(4,1)S(1)} %fusion.8), kind=kOutput, calls=%fused_computation.15 | convolution fusion | flops 1227363456 | bytes 24952832 | tf_op jit(solution)/shard_map/hqk,khd->qhd/dot_general | solution.py:56
  174.6 0.0 copy-start.3
  174.6 0.0 copy-start.5
  174.6 0.0 copy-start.1
  174.7 11.7 %convolution_convert_fusion = bf16[256,4096]{1,0:T(8,128)(2,1)} fusion(bf16[256,2048]{0,1:T(8,128)(2,1)S(1)} %bitcast.58, bf16[2048,4096]{1,0:T(8,128)(2,1)} %param.11), kind=kOutput, calls=%fused_computation.10 | convolution fusion | flops 4296015872 | bytes 19922944 | tf_op jit(solution)/shard_map/dot_general | solution.py:80
  186.4 0.0 reduce-scatter.2.cloned.1.call-update
  186.4 135.4 %reduce-scatter.2.cloned.1.call-done = bf16[256,2048]{1,0:T(8,128)(2,1)} async-done(((bf16[256,4096]{1,0:T(8,128)(2,1)}), bf16[256,2048]{1,0:T(8,128)(2,1)}) %reduce-scatter.2.cloned.1.call-update) | async-done | bytes 1048592 | tf_op jit(solution)/shard_map/reduce_scatter | solution.py:81
  321.8 1.6 multiply_reduce_fusion
  323.5 2.5 psum.7
  325.9 3.2 multiply_convert_fusion
  (23 shorter events, 0.1 us)
Async XLA Ops:
  7.2 128.1 %copy-start = (bf16[256,2048]{1,0:T(8,128)(2,1)S(1)}, bf16[256,2048]{1,0:T(8,128)(2,1)}, u32[]{:S(2)}) copy-start(bf16[256,2048]{1,0:T(8,128)(2,1)} %param.7) | copy-start | bytes 3145732
  7.2 100.7 %copy-start.4 = (bf16[256,2048]{1,0:T(8,128)(2,1)S(1)}, bf16[256,2048]{1,0:T(8,128)(2,1)}, u32[]{:S(2)}) copy-start(bf16[256,2048]{1,0:T(8,128)(2,1)} %param.9) | copy-start | bytes 3145732
  7.2 314.6 %reduce-scatter.2.cloned.1.call-start = ((), (), s32[]{:S(2)}) async-start(), calls=%async_computation.1 | async-start | bytes 3145728 | tf_op jit(solution)/shard_map/reduce_scatter | solution.py:81
  8.9 112.3 %collective-permute-start.7 = (bf16[256,2048]{0,1:T(8,128)(2,1)S(1)}, bf16[256,2048]{0,1:T(8,128)(2,1)}, u32[]{:S(2)}, u32[]{:S(2)}) collective-permute-start(bf16[256,2048]{0,1:T(8,128)(2,1)S(1)} %copy.26), channel_id=1, source_target_pairs={{0,1},{1,2},{2,3},{3,4},{4,5},{5,6},{6,7},{7,8},{8,9},{9,10},{10,1... | collective-permute-start | bytes 3145736 | tf_op jit(solution)/shard_map/ppermute | solution.py:18
  13.8 106.1 %collective-permute-start.6 = (bf16[256,2048]{0,1:T(8,128)(2,1)S(1)}, bf16[256,2048]{0,1:T(8,128)(2,1)}, u32[]{:S(2)}, u32[]{:S(2)}) collective-permute-start(bf16[256,2048]{0,1:T(8,128)(2,1)S(1)} %copy.26), channel_id=1, source_target_pairs={{0,2},{1,3},{2,4},{3,5},{4,6},{5,7},{6,8},{7,9},{8,10},{9,11},{10,... | collective-permute-start | bytes 3145736 | tf_op jit(solution)/shard_map/ppermute | solution.py:18
  18.3 92.9 %collective-permute-start.5 = (bf16[256,2048]{0,1:T(8,128)(2,1)S(1)}, bf16[256,2048]{0,1:T(8,128)(2,1)}, u32[]{:S(2)}, u32[]{:S(2)}) collective-permute-start(bf16[256,2048]{0,1:T(8,128)(2,1)S(1)} %copy.26), channel_id=1, source_target_pairs={{0,3},{1,4},{2,5},{3,6},{4,7},{5,8},{6,9},{7,10},{8,11},{9,12},{10... | collective-permute-start | bytes 3145736 | tf_op jit(solution)/shard_map/ppermute | solution.py:18
  24.2 83.7 %collective-permute-start = (bf16[128,2048]{1,0:T(8,128)(2,1)}, bf16[128,2048]{1,0:T(8,128)(2,1)}, u32[]{:S(2)}, u32[]{:S(2)}) collective-permute-start(bf16[128,2048]{1,0:T(8,128)(2,1)} %slice.6), channel_id=1, source_target_pairs={{0,4},{1,5},{2,6},{3,7},{4,8},{5,9},{6,10},{7,11},{8,12},{9,13},{1... | collective-permute-start | bytes 1572872 | tf_op jit(solution)/shard_map/ppermute | solution.py:18
  28.0 77.4 %collective-permute-start.4 = (bf16[128,2048]{0,1:T(8,128)(2,1)}, bf16[128,2048]{0,1:T(8,128)(2,1)}, u32[]{:S(2)}, u32[]{:S(2)}) collective-permute-start(bf16[128,2048]{0,1:T(8,128)(2,1)} %slice.8), channel_id=1, source_target_pairs={{0,4},{1,5},{2,6},{3,7},{4,8},{5,9},{6,10},{7,11},{8,12},{9,13},{1... | collective-permute-start | bytes 1572872 | tf_op jit(solution)/shard_map/ppermute | solution.py:18
  105.4 37.8 %collective-permute-start.2 = (bf16[256,2048]{1,0:T(8,128)(2,1)}, bf16[256,2048]{1,0:T(8,128)(2,1)S(1)}, u32[]{:S(2)}, u32[]{:S(2)}) collective-permute-start(bf16[256,2048]{1,0:T(8,128)(2,1)} %param.9), channel_id=1, source_target_pairs={{0,2},{1,3},{2,4},{3,5},{4,6},{5,7},{6,8},{7,9},{8,10},{9,11},{10,... | collective-permute-start | bytes 3145736 | tf_op jit(solution)/shard_map/ppermute | solution.py:18
  107.9 26.2 %collective-permute-start.1 = (bf16[256,2048]{1,0:T(8,128)(2,1)S(1)}, bf16[256,2048]{1,0:T(8,128)(2,1)S(1)}, u32[]{:S(2)}, u32[]{:S(2)}) collective-permute-start(bf16[256,2048]{1,0:T(8,128)(2,1)S(1)} %copy-done.4), channel_id=1, source_target_pairs={{0,3},{1,4},{2,5},{3,6},{4,7},{5,8},{6,9},{7,10},{8,11},{9,12},{10... | collective-permute-start | bytes 3145736 | tf_op jit(solution)/shard_map/ppermute | solution.py:18
  111.1 41.3 %collective-permute-start.3 = (bf16[256,2048]{1,0:T(8,128)(2,1)S(1)}, bf16[256,2048]{1,0:T(8,128)(2,1)}, u32[]{:S(2)}, u32[]{:S(2)}) collective-permute-start(bf16[256,2048]{1,0:T(8,128)(2,1)S(1)} %copy-done.4), channel_id=1, source_target_pairs={{0,1},{1,2},{2,3},{3,4},{4,5},{5,6},{6,7},{7,8},{8,9},{9,10},{10,1... | collective-permute-start | bytes 3145736 | tf_op jit(solution)/shard_map/ppermute | solution.py:18
  122.6 20.6 %copy-start.2 = (bf16[1152,2048]{0,1:T(8,128)(2,1)}, bf16[1152,2048]{0,1:T(8,128)(2,1)S(1)}, u32[]{:S(2)}) copy-start(bf16[1152,2048]{0,1:T(8,128)(2,1)S(1)} %constant_dynamic-update-slice_fusion.5) | copy-start | bytes 14155780
  174.6 147.2 %copy-start.3 = (bf16[256,2048]{1,0:T(8,128)(2,1)S(1)}, bf16[256,2048]{1,0:T(8,128)(2,1)}, u32[]{:S(2)}) copy-start(bf16[256,2048]{1,0:T(8,128)(2,1)} %param.12) | copy-start | bytes 3145732
  174.6 151.3 %copy-start.5 = (f32[2048]{0:T(1024)S(1)}, f32[2048]{0:T(1024)}, u32[]{:S(2)}) copy-start(f32[2048]{0:T(1024)} %param.13) | copy-start | bytes 24580
  174.6 154.5 %copy-start.1 = (bf16[256,2048]{1,0:T(8,128)(2,1)S(1)}, bf16[256,2048]{1,0:T(8,128)(2,1)}, u32[]{:S(2)}) copy-start(bf16[256,2048]{1,0:T(8,128)(2,1)} %param.7) | copy-start | bytes 3145732
Sparse Core Ops, SparseCore 0:
  186.5 135.2 reduce-scatter.1
where the time goes:
time: 337 us; the launch traced here: 336 us
  waiting for transfers between devices  220 us (65%)
  matrix products  39.9 us (12%)
  starting transfers between devices  29.5 us (9%)
  local copies, waits for them, and re-layouts  24 us (7%)
  between operations  14.3 us (4%)
  other arithmetic  6.01 us (2%)
    reduce_scatter x1, waiting for transfers between devices, shards(): lax.psum_scatter(partial_value.astype(jnp.bfloat16), 'section', scatter_d...  135 us
    ppermute x8, waiting for transfers between devices, from_behind(): return lax.ppermute(block, axis, route)  84.5 us
    ppermute x8, starting transfers between devices, from_behind(): return lax.ppermute(block, axis, route)  29.5 us
    unnamed x27, local copies, waits for them, and re-layouts  13.3 us
    dot_general x1, matrix products, attend(): jnp.einsum('hqk,khd->qhd', weights, value_group, preferred_element_type=j...  12 us
    dot_general x1, matrix products, shards(): jnp.dot(attended, out_weight, preferred_element_type=jnp.float32)  11.7 us
    sub x1, matrix products, attend(): exponent = jnp.exp(scores - largest)  8.2 us
    dot_general x1, matrix products, attend(): jnp.einsum('qhd,khd->hqk', query_group, key_group, preferred_element_type...  7.92 us
  transfers between devices with their start and end apart: 9, of which 3 were waited for; matrix products, arithmetic and copies ran while one was open for 9% of the time, Pallas kernels for 0%

commit v1 on v0

v1 whole, which is shorter than its diff:
```python
import math

import jax
import jax.numpy as jnp
from jax import lax
from jax.experimental import pallas as pl
from jax.experimental.pallas import tpu as pltpu
from jax.sharding import PartitionSpec as P

D = 4096
HALF = 2048
HEAD_DIM = 128
BLOCK = 128
WINDOW = 8
ROWS = 256
RING = 4
SLOTS = 1
WIDTH = 512 // SLOTS
HIDE = -3e38
VMEM = 12 * 1024 * 1024


def ring_shift(array, d):
    route = [(i, (i // RING) * RING + (i + d) % RING) for i in range(128)]
    return lax.ppermute(array, "seq", route)


def next_row(array):
    return lax.ppermute(array, "seq", [(i, i + RING) for i in range(128 - RING)])


def other_core(array):
    return lax.ppermute(array, "section", [(0, 1), (1, 0)])


def after(array, *others):
    return lax.optimization_barrier((array,) + others)[0]


def attend_kernel(order, x_ref, *refs):
    own = refs[0:4]
    halo = refs[4:8]
    count = len(order)
    qs = refs[8 : 8 + count]
    outs = refs[8 + count : 8 + 2 * count]
    kbuf, vbuf = refs[8 + 2 * count :]
    x = x_ref[0]
    for d in range(RING):
        j = (x + RING - d) & 3
        far = pl.multiple_of(j * ROWS, ROWS)
        near = pl.multiple_of(j * ROWS + RING * ROWS, ROWS)
        kbuf[pl.ds(far, ROWS), :] = halo[d][0:ROWS, :]
        vbuf[pl.ds(far, ROWS), :] = halo[d][ROWS : 2 * ROWS, :]
        kbuf[pl.ds(near, ROWS), :] = own[d][0:ROWS, :]
        vbuf[pl.ds(near, ROWS), :] = own[d][ROWS : 2 * ROWS, :]
    row = lax.broadcasted_iota(jnp.int32, (BLOCK, BLOCK), 0)
    col = lax.broadcasted_iota(jnp.int32, (BLOCK, BLOCK), 1)
    causal = col <= row
    factor = math.log2(math.e) / math.sqrt(HEAD_DIM)
    for index, d in enumerate(order):
        j = (x + RING - d) & 3
        for r in range(2):
            start = pl.multiple_of((2 * j + r + 1) * BLOCK, BLOCK)
            span = pl.ds(start, WINDOW * BLOCK)
            q = qs[index][r * BLOCK : (r + 1) * BLOCK, :]
            hide = qs[index][ROWS : ROWS + 16, :].astype(jnp.float32)
            s = lax.dot_general(
                q, kbuf[span, :], (((1,), (1,)), ((), ())), preferred_element_type=jnp.float32
            )
            parts = []
            for i in range(WINDOW - 1):
                line = hide[r * 8 + i : r * 8 + i + 1, :]
                parts.append(s[:, i * BLOCK : (i + 1) * BLOCK] + line)
            parts.append(jnp.where(causal, s[:, (WINDOW - 1) * BLOCK :], HIDE))
            top = parts[0]
            for part in parts[1:]:
                top = jnp.maximum(top, part)
            top = jnp.max(top, axis=1, keepdims=True)
            parts = [jnp.exp2((part - top) * factor) for part in parts]
            total = parts[0]
            for part in parts[1:]:
                total = total + part
            total = jnp.sum(total, axis=1, keepdims=True)
            p = jnp.concatenate([part.astype(jnp.bfloat16) for part in parts], axis=1)
            o = jnp.dot(p, vbuf[span, :], preferred_element_type=jnp.float32)
            outs[index][r * BLOCK : (r + 1) * BLOCK, :] = (o / total).astype(jnp.bfloat16)


def attend(x, own, halo, qs, order):
    count = len(order)
    piece = pl.BlockSpec((2 * ROWS, HEAD_DIM), lambda h, x: (0, h))
    query = pl.BlockSpec((ROWS + 16, HEAD_DIM), lambda h, x: (0, h))
    result = pl.BlockSpec((ROWS, HEAD_DIM), lambda h, x: (0, h))
    return pl.pallas_call(
        lambda *refs: attend_kernel(order, *refs),
        out_shape=[jax.ShapeDtypeStruct((ROWS, WIDTH), jnp.bfloat16)] * count,
        grid_spec=pltpu.PrefetchScalarGridSpec(
            num_scalar_prefetch=1,
            grid=(WIDTH // HEAD_DIM,),
            in_specs=[piece] * 8 + [query] * count,
            out_specs=[result] * count,
            scratch_shapes=[pltpu.VMEM((2 * RING * ROWS, HEAD_DIM), jnp.bfloat16)] * 2,
        ),
        compiler_params=pltpu.CompilerParams(vmem_limit_bytes=VMEM),
        cost_estimate=pl.CostEstimate(
            flops=count * 1100000000 // 2 // SLOTS,
            bytes_accessed=5000000 // SLOTS,
            transcendentals=count * 1000000 // SLOTS,
        ),
        name="attend",
    )(x, *own, *halo, *qs)


TILE = 512


def project_kernel(x_ref, *refs):
    count = (len(refs) - 1) // 2
    total = None
    for o, w in zip(refs[:count], refs[count : 2 * count]):
        term = jnp.dot(o[...], w[...], preferred_element_type=jnp.float32)
        total = term if total is None else total + term
    refs[-1][...] = total.astype(jnp.bfloat16)


def project(x, pieces, weight):
    keys = list(pieces)
    values = [pieces[key] for key in keys]

    def weight_block(d, s):
        return pl.BlockSpec((WIDTH, TILE), lambda n, x: (((x[0] + d) & 3) * SLOTS + s, n))

    return pl.pallas_call(
        project_kernel,
        out_shape=jax.ShapeDtypeStruct((ROWS, D), jnp.bfloat16),
        grid_spec=pltpu.PrefetchScalarGridSpec(
            num_scalar_prefetch=1,
            grid=(D // TILE,),
            in_specs=[pl.BlockSpec((ROWS, WIDTH), lambda n, x: (0, 0)) for _ in keys]
            + [weight_block(d, s) for d, s in keys],
            out_specs=pl.BlockSpec((ROWS, TILE), lambda n, x: (0, n)),
        ),
        compiler_params=pltpu.CompilerParams(vmem_limit_bytes=VMEM),
        cost_estimate=pl.CostEstimate(
            flops=2 * ROWS * HALF * D, bytes_accessed=20000000, transcendentals=0
        ),
        name="project",
    )(x, *values, *([weight] * len(keys)))


STRIP = 64


def finish_kernel(s_ref, near, far, hidden_own, hidden_other, gain, stream_ref, normed_ref):
    side = pl.multiple_of(s_ref[0] * HALF, HALF)
    away = pl.multiple_of((1 - s_ref[0]) * HALF, HALF)

    def stream_of(columns, hidden):
        total = near[:, columns].astype(jnp.float32) + far[:, columns].astype(jnp.float32)
        return hidden[...].astype(jnp.float32) + total

    mine = stream_of(pl.ds(side, HALF), hidden_own)
    rest = stream_of(pl.ds(away, HALF), hidden_other)
    squares = jnp.sum(mine * mine + rest * rest, axis=1, keepdims=True)
    factor = lax.rsqrt(squares / D + 1e-06)
    stream_ref[...] = mine.astype(jnp.bfloat16)
    normed_ref[...] = (mine * factor * gain[...]).astype(jnp.bfloat16)


def finish(section, near, far, hidden_own, hidden_other, gain):
    whole = pl.BlockSpec((STRIP, D), lambda i, s: (i, 0))
    half = pl.BlockSpec((STRIP, HALF), lambda i, s: (i, 0))
    return pl.pallas_call(
        finish_kernel,
        out_shape=[jax.ShapeDtypeStruct((ROWS, HALF), jnp.bfloat16)] * 2,
        grid_spec=pltpu.PrefetchScalarGridSpec(
            num_scalar_prefetch=1,
            grid=(ROWS // STRIP,),
            in_specs=[whole, whole, half, half, pl.BlockSpec((1, HALF), lambda i, s: (0, 0))],
            out_specs=[half, half],
        ),
        compiler_params=pltpu.CompilerParams(vmem_limit_bytes=VMEM),
        cost_estimate=pl.CostEstimate(flops=10000000, bytes_accessed=8000000, transcendentals=256),
        name="finish",
    )(section, near, far, hidden_own, hidden_other, gain.reshape(1, HALF))


def hide_rows(block_pattern, shard):
    back = WINDOW - 1 - jnp.arange(WINDOW, dtype=jnp.int32)[None, :]
    query_block = shard * 2 + jnp.arange(2, dtype=jnp.int32)[:, None]
    allowed = (block_pattern[:, ::-1] == 1) & (query_block - back >= 0)
    flags = jnp.where(allowed, 0.0, HIDE).astype(jnp.bfloat16).reshape(16, 1)
    return jnp.broadcast_to(flags, (16, WIDTH))


def shards(queries, key_rows, value_rows, block_pattern, out_weight, hidden, norm_gain):
    shard = lax.axis_index("seq")
    section = lax.axis_index("section").astype(jnp.int32)
    x = (shard % RING).astype(jnp.int32)
    hide = hide_rows(block_pattern, shard)

    def cut(array, d, s):
        begin = ((x + d) % RING) * 512 + s * WIDTH
        return lax.dynamic_slice(array, (jnp.int32(0), begin), (ROWS, WIDTH))

    def pack_kv(d, s):
        return jnp.concatenate([cut(key_rows, d, s), cut(value_rows, d, s)], 0)

    def pack_q(d, s):
        return jnp.concatenate([cut(queries, d, s), hide], 0)

    hidden_other = other_core(hidden)
    pieces = {}
    for s in range(SLOTS):
        own, halo, qs = [None] * 4, [None] * 4, [None] * 4
        own[0] = pack_kv(0, s)
        for d in (1, 3):
            own[d] = ring_shift(pack_kv(d, s), d)
        halo[0] = next_row(own[0])
        own[2] = ring_shift(after(pack_kv(2, s), own[1], own[3]), 2)
        for d in (1, 3):
            qs[d] = ring_shift(after(pack_q(d, s), own[1], own[3]), d)
        for d in (1, 3, 2):
            halo[d] = next_row(own[d])
        qs[2] = ring_shift(after(pack_q(2, s), own[2], hidden_other), 2)
        qs[0] = pack_q(0, s)
        xs = x.reshape(1)
        for order in ((2, 1), (3, 0)):
            outs = attend(xs, own, halo, [qs[d] for d in order], order)
            for d, out in zip(order, outs):
                pieces[d, s] = ring_shift(out, -d) if d else out
    near = project(x.reshape(1), pieces, out_weight)
    far = other_core(near)
    return tuple(
        finish(section.reshape(1), near, far, hidden, hidden_other, norm_gain)
    )


def solution(mesh):
    placed = (
        P("seq", "section"),
        P("seq", "section"),
        P("seq", "section"),
        P("seq", None),
        P("section", None),
        P("seq", "section"),
        P("section"),
    )
    return jax.shard_map(
        shards,
        mesh=mesh,
        in_specs=placed,
        out_specs=(P("seq", "section"), P("seq", "section")),
        check_vma=False,
    )
```

time: 337 us -> 124 us (0.37)
  the two profiles are of different devices: /device:TPU:1 before, /device:TPU:131 now
where the time goes in v1:
time: 124 us
  waiting for transfers between devices  57.9 us (47%)
  starting transfers between devices  27.1 us (22%)
  Pallas kernels  27 us (22%)
  local copies, waits for them, and re-layouts  8.66 us (7%)
  other arithmetic  2.21 us (2%)
    ppermute x9, waiting for transfers between devices, ring_shift(): return lax.ppermute(array, 'seq', route)  28.4 us
    ppermute x4, waiting for transfers between devices, next_row(): lax.ppermute(array, 'seq', [(i, i + RING) for i in range(128 - RING)])  25.6 us
    pallas_call x2, Pallas kernels, attend(): pl.pallas_call(lambda *refs: attend_kernel(order, *refs), out_shape=[jax....  15.2 us
    ppermute x4, starting transfers between devices, next_row(): lax.ppermute(array, 'seq', [(i, i + RING) for i in range(128 - RING)])  12.5 us
    ppermute x9, starting transfers between devices, ring_shift(): return lax.ppermute(array, 'seq', route)  11.8 us
    pallas_call x1, Pallas kernels, project(): pl.pallas_call(project_kernel, out_shape=jax.ShapeDtypeStruct((ROWS, D),...  7.24 us
    unnamed x10, local copies, waits for them, and re-layouts  6.13 us
    pallas_call x1, Pallas kernels, finish(): pl.pallas_call(finish_kernel, out_shape=[jax.ShapeDtypeStruct((ROWS, HALF...  4.55 us
  transfers between devices with their start and end apart: 15, of which 10 were waited for; matrix products, arithmetic and copies ran while one was open for 2% of the time, Pallas kernels for 12%

profile of v1, /device:TPU:131, one launch (start us, length us, event | category | flops | bytes accessed | tf_op | source)
XLA Modules:
  0.0 123.7 jit_solution(1998161221886592296)
XLA Ops:
  0.6 0.0 copy-start.3
  0.6 0.0 copy-start.2
  0.7 1.4 %constant_dynamic-slice_fusion.5 = (bf16[256,512]{1,0:T(8,128)(2,1)S(1)}, bf16[256,512]{1,0:T(8,128)(2,1)S(1)}, bf16[256,512]{1,0:T(8,128)(2,1)S(1)}, bf16[256,512]{1,0:T(8,128)(2,1)S(1)}) fusion(bf16[256,2048]{1,0:T(8,128)(2,1)} %param.8, s32[]{:T(128)S(6)} %select_n.71, s32[]{:T(128)S(6)} %select_n.67, s32[]{:T(128)S(6)} %select_n.65, s32[]{:T(128)S(6)} %select_n.69), kind=kLoop, calls=%fused_computation.13 | loop fusion | bytes 2097168 | tf_op jit(solution)/shard_map/dynamic_slice | solution.py:204
  2.1 0.0 copy-done.3
  2.2 0.3 copy-done.2
  2.5 0.9 constant_dynamic-slice_fusion
  3.5 0.3 collective-permute-start.1
  3.8 1.3 %collective-permute-start = (bf16[512,512]{1,0:T(8,128)(2,1)S(1)}, bf16[512,512]{1,0:T(8,128)(2,1)S(1)}, u32[]{:S(2)}, u32[]{:S(2)}) collective-permute-start(bf16[512,512]{1,0:T(8,128)(2,1)S(1)} %pad_maximum_fusion.1), channel_id=1, source_target_pairs={{0,1},{1,2},{2,3},{3,0},{4,5},{5,6},{6,7},{7,4},{8,9},{9,10},{10,1... | collective-permute-start | bytes 1572872 | tf_op jit(solution)/shard_map/ppermute | solution.py:25
  5.1 1.2 collective-permute-start.7
  6.4 0.8 pad_maximum_fusion.2
  7.2 9.1 %collective-permute-done.1.refs_4_ = bf16[512,512]{1,0:T(8,128)(2,1)S(1)} collective-permute-done((bf16[512,512]{1,0:T(8,128)(2,1)S(1)}, bf16[512,512]{1,0:T(8,128)(2,1)S(1)}, u32[]{:S(2)}, u32[]{:S(2)}) %collective-permute-start.1) | collective-permute-done | bytes 524320 | tf_op jit(solution)/shard_map/ppermute | solution.py:25
  16.3 1.4 %collective-permute-done.refs_2_ = bf16[512,512]{1,0:T(8,128)(2,1)S(1)} collective-permute-done((bf16[512,512]{1,0:T(8,128)(2,1)S(1)}, bf16[512,512]{1,0:T(8,128)(2,1)S(1)}, u32[]{:S(2)}, u32[]{:S(2)}) %collective-permute-start) | collective-permute-done | bytes 524320 | tf_op jit(solution)/shard_map/ppermute | solution.py:25
  17.7 1.7 %collective-permute-start.2 = (bf16[512,512]{1,0:T(8,128)(2,1)}, bf16[512,512]{1,0:T(8,128)(2,1)S(1)}, u32[]{:S(2)}, u32[]{:S(2)}) collective-permute-start(bf16[512,512]{1,0:T(8,128)(2,1)} %pad_maximum_fusion.2), channel_id=1, source_target_pairs={{0,2},{1,3},{2,0},{3,1},{4,6},{5,7},{6,4},{7,5},{8,10},{9,11},{10,... | collective-permute-start | bytes 1572872 | tf_op jit(solution)/shard_map/ppermute | solution.py:25
  19.4 3.2 %collective-permute-start.3 = (bf16[512,512]{1,0:T(8,128)(2,1)S(1)}, bf16[512,512]{1,0:T(8,128)(2,1)S(1)}, u32[]{:S(2)}, u32[]{:S(2)}) collective-permute-start(bf16[512,512]{1,0:T(8,128)(2,1)S(1)} %pad_maximum_fusion.refs_1_), channel_id=1, source_target_pairs={{0,4},{1,5},{2,6},{3,7},{4,8},{5,9},{6,10},{7,11},{8,12},{9,13},{1... | collective-permute-start | bytes 1572872 | tf_op jit(solution)/shard_map/ppermute | solution.py:29
  22.7 0.0 copy-done.4
  22.7 0.1 rev.3
  22.8 0.1 fusion
  22.9 0.1 reshape.29
  22.9 3.2 %collective-permute-start.6 = (bf16[512,512]{1,0:T(8,128)(2,1)S(1)}, bf16[512,512]{1,0:T(8,128)(2,1)S(1)}, u32[]{:S(2)}, u32[]{:S(2)}) collective-permute-start(bf16[512,512]{1,0:T(8,128)(2,1)S(1)} %collective-permute-done.1.refs_4_), channel_id=1, source_target_pairs={{0,4},{1,5},{2,6},{3,7},{4,8},{5,9},{6,10},{7,11},{8,12},{9,13},{1... | collective-permute-start | bytes 1572872 | tf_op jit(solution)/shard_map/ppermute | solution.py:29
  26.1 2.9 %collective-permute-start.4 = (bf16[512,512]{1,0:T(8,128)(2,1)S(1)}, bf16[512,512]{1,0:T(8,128)(2,1)S(1)}, u32[]{:S(2)}, u32[]{:S(2)}) collective-permute-start(bf16[512,512]{1,0:T(8,128)(2,1)S(1)} %collective-permute-done.refs_2_), channel_id=1, source_target_pairs={{0,4},{1,5},{2,6},{3,7},{4,8},{5,9},{6,10},{7,11},{8,12},{9,13},{1... | collective-permute-start | bytes 1572872 | tf_op jit(solution)/shard_map/ppermute | solution.py:29
  29.1 2.3 %collective-permute-done.2.refs_3_ = bf16[512,512]{1,0:T(8,128)(2,1)S(1)} collective-permute-done((bf16[512,512]{1,0:T(8,128)(2,1)}, bf16[512,512]{1,0:T(8,128)(2,1)S(1)}, u32[]{:S(2)}, u32[]{:S(2)}) %collective-permute-start.2) | collective-permute-done | bytes 524320 | tf_op jit(solution)/shard_map/ppermute | solution.py:25
  31.3 3.2 %collective-permute-start.5 = (bf16[512,512]{1,0:T(8,128)(2,1)S(1)}, bf16[512,512]{1,0:T(8,128)(2,1)S(1)}, u32[]{:S(2)}, u32[]{:S(2)}) collective-permute-start(bf16[512,512]{1,0:T(8,128)(2,1)S(1)} %collective-permute-done.2.refs_3_), channel_id=1, source_target_pairs={{0,4},{1,5},{2,6},{3,7},{4,8},{5,9},{6,10},{7,11},{8,12},{9,13},{1... | collective-permute-start | bytes 1572872 | tf_op jit(solution)/shard_map/ppermute | solution.py:29
  34.5 1.2 pad_maximum_fusion.7
  35.7 0.0 collective-permute-done.7.hidden_other
  35.7 2.1 %collective-permute-start.12 = (bf16[272,512]{1,0:T(8,128)(2,1)S(1)}, bf16[272,512]{1,0:T(8,128)(2,1)S(1)}, u32[]{:S(2)}, u32[]{:S(2)}) collective-permute-start(bf16[272,512]{1,0:T(8,128)(2,1)S(1)} %get-tuple-element.15), channel_id=1, source_target_pairs={{0,3},{1,0},{2,1},{3,2},{4,7},{5,4},{6,5},{7,6},{8,11},{9,8},{10,9... | collective-permute-start | bytes 835592 | tf_op jit(solution)/shard_map/ppermute | solution.py:25
  37.8 0.0 collective-permute-done.3.refs_5_
  37.8 0.0 collective-permute-start.9
  37.9 3.7 %collective-permute-done.12.refs_9_ = bf16[272,512]{1,0:T(8,128)(2,1)S(1)} collective-permute-done((bf16[272,512]{1,0:T(8,128)(2,1)S(1)}, bf16[272,512]{1,0:T(8,128)(2,1)S(1)}, u32[]{:S(2)}, u32[]{:S(2)}) %collective-permute-start.12) | collective-permute-done | bytes 278560 | tf_op jit(solution)/shard_map/ppermute | solution.py:25
  41.5 2.9 %collective-permute-start.8 = (bf16[272,512]{1,0:T(8,128)(2,1)S(1)}, bf16[272,512]{1,0:T(8,128)(2,1)S(1)}, u32[]{:S(2)}, u32[]{:S(2)}) collective-permute-start(bf16[272,512]{1,0:T(8,128)(2,1)S(1)} %get-tuple-element.11), channel_id=1, source_target_pairs={{0,2},{1,3},{2,0},{3,1},{4,6},{5,7},{6,4},{7,5},{8,10},{9,11},{10,... | collective-permute-start | bytes 835592 | tf_op jit(solution)/shard_map/ppermute | solution.py:25
  44.4 3.1 %collective-permute-done.6.refs_8_ = bf16[512,512]{1,0:T(8,128)(2,1)S(1)} collective-permute-done((bf16[512,512]{1,0:T(8,128)(2,1)S(1)}, bf16[512,512]{1,0:T(8,128)(2,1)S(1)}, u32[]{:S(2)}, u32[]{:S(2)}) %collective-permute-start.6) | collective-permute-done | bytes 524320 | tf_op jit(solution)/shard_map/ppermute | solution.py:29
  47.5 11.2 %collective-permute-done.4.refs_6_ = bf16[512,512]{1,0:T(8,128)(2,1)S(1)} collective-permute-done((bf16[512,512]{1,0:T(8,128)(2,1)S(1)}, bf16[512,512]{1,0:T(8,128)(2,1)S(1)}, u32[]{:S(2)}, u32[]{:S(2)}) %collective-permute-start.4) | collective-permute-done | bytes 524320 | tf_op jit(solution)/shard_map/ppermute | solution.py:29
  58.7 11.2 %collective-permute-done.5.refs_7_ = bf16[512,512]{1,0:T(8,128)(2,1)S(1)} collective-permute-done((bf16[512,512]{1,0:T(8,128)(2,1)S(1)}, bf16[512,512]{1,0:T(8,128)(2,1)S(1)}, u32[]{:S(2)}, u32[]{:S(2)}) %collective-permute-start.5) | collective-permute-done | bytes 524320 | tf_op jit(solution)/shard_map/ppermute | solution.py:29
  70.0 7.6 %attend.3 = (bf16[256,512]{1,0:T(8,128)(2,1)S(1)}, bf16[256,512]{1,0:T(8,128)(2,1)S(1)}) custom-call(s32[1]{0:T(128)} %bitcast.1.refs_0_.x_ref, bf16[512,512]{1,0:T(8,128)(2,1)S(1)} %pad_maximum_fusion.refs_1_, bf16[512,512]{1,0:T(8,128)(2,1)S(1)} %collective-permute-done.refs_2_, bf16[512,512]{1,0:T(8,128)(2,1)S(1)} %collective-permute-done.2.refs_3_, ...), custom_call_target="tpu_custom_call" | custom-call | flops 1100000000 | bytes 5000000 | tf_op jit(solution)/shard_map/attend/pallas_call | solution.py:94
  77.5 1.6 %collective-permute-start.13 = (bf16[256,512]{1,0:T(8,128)(2,1)S(1)}, bf16[256,512]{1,0:T(8,128)(2,1)S(1)}, u32[]{:S(2)}, u32[]{:S(2)}) collective-permute-start(bf16[256,512]{1,0:T(8,128)(2,1)S(1)} %get-tuple-element.16), channel_id=1, source_target_pairs={{0,1},{1,2},{2,3},{3,0},{4,5},{5,6},{6,7},{7,4},{8,9},{9,10},{10,1... | collective-permute-start | bytes 786440 | tf_op jit(solution)/shard_map/ppermute | solution.py:25
  79.2 0.0 collective-permute-done.9.refs_10_
  79.2 0.0 collective-permute-done.8.refs_9_
  79.2 7.6 %attend.2 = (bf16[256,512]{1,0:T(8,128)(2,1)S(1)}, bf16[256,512]{1,0:T(8,128)(2,1)S(1)}) custom-call(s32[1]{0:T(128)} %bitcast.1.refs_0_.x_ref, bf16[512,512]{1,0:T(8,128)(2,1)S(1)} %pad_maximum_fusion.refs_1_, bf16[512,512]{1,0:T(8,128)(2,1)S(1)} %collective-permute-done.refs_2_, bf16[512,512]{1,0:T(8,128)(2,1)S(1)} %collective-permute-done.2.refs_3_, ...), custom_call_target="tpu_custom_call" | custom-call | flops 1100000000 | bytes 5000000 | tf_op jit(solution)/shard_map/attend/pallas_call | solution.py:94
  86.8 1.0 collective-permute-start.10
  87.7 1.0 collective-permute-start.11
  88.7 0.0 collective-permute-done.13.refs_2_
  88.7 5.0 %collective-permute-done.10.refs_0_ = bf16[256,512]{1,0:T(8,128)(2,1)S(1)} collective-permute-done((bf16[256,512]{1,0:T(8,128)(2,1)S(1)}, bf16[256,512]{1,0:T(8,128)(2,1)S(1)}, u32[]{:S(2)}, u32[]{:S(2)}) %collective-permute-start.10) | collective-permute-done | bytes 262176 | tf_op jit(solution)/shard_map/ppermute | solution.py:25
  93.7 6.9 %collective-permute-done.11.refs_1_ = bf16[256,512]{1,0:T(8,128)(2,1)S(1)} collective-permute-done((bf16[256,512]{1,0:T(8,128)(2,1)S(1)}, bf16[256,512]{1,0:T(8,128)(2,1)S(1)}, u32[]{:S(2)}, u32[]{:S(2)}) %collective-permute-start.11) | collective-permute-done | bytes 262176 | tf_op jit(solution)/shard_map/ppermute | solution.py:25
  100.6 5.8 %copy-done = bf16[2048,4096]{1,0:T(8,128)(2,1)S(1)} copy-done((bf16[2048,4096]{1,0:T(8,128)(2,1)S(1)}, bf16[2048,4096]{1,0:T(8,128)(2,1)}, u32[]{:S(2)}) %copy-start) | copy-done | bytes 16777240
  106.4 7.2 %project.1.near = bf16[256,4096]{1,0:T(8,128)(2,1)S(1)} custom-call(s32[1]{0:T(128)} %bitcast.1.refs_0_.x_ref, bf16[256,512]{1,0:T(8,128)(2,1)S(1)} %collective-permute-done.10.refs_0_, bf16[256,512]{1,0:T(8,128)(2,1)S(1)} %collective-permute-done.11.refs_1_, bf16[256,512]{1,0:T(8,128)(2,1)S(1)} %collective-permute-done.13.refs_2_, ...), custom_call_target="tpu_custom_call" | custom-call | flops 4294967296 | bytes 20000000 | tf_op jit(solution)/shard_map/project/pallas_call | solution.py:133
  113.6 1.6 %collective-permute-start.14 = (bf16[256,4096]{1,0:T(8,128)(2,1)S(1)}, bf16[256,4096]{1,0:T(8,128)(2,1)}, u32[]{:S(2)}, u32[]{:S(2)}) collective-permute-start(bf16[256,4096]{1,0:T(8,128)(2,1)S(1)} %project.1.near), channel_id=1, source_target_pairs={{0,128},{128,0},{1,129},{129,1},{2,130},{130,2},{3,131},{131,3},{4... | collective-permute-start | bytes 6291464 | tf_op jit(solution)/shard_map/ppermute | solution.py:33
  115.2 3.9 %collective-permute-done.14.far = bf16[256,4096]{1,0:T(8,128)(2,1)} collective-permute-done((bf16[256,4096]{1,0:T(8,128)(2,1)S(1)}, bf16[256,4096]{1,0:T(8,128)(2,1)}, u32[]{:S(2)}, u32[]{:S(2)}) %collective-permute-start.14) | collective-permute-done | bytes 2097184 | tf_op jit(solution)/shard_map/ppermute | solution.py:33
  119.1 0.0 copy-done.1
  119.1 4.6 %finish.1 = (bf16[256,2048]{1,0:T(8,128)(2,1)}, bf16[256,2048]{1,0:T(8,128)(2,1)}) custom-call(s32[1]{0:T(128)} %bitcast.s_ref, bf16[256,4096]{1,0:T(8,128)(2,1)S(1)} %project.1.near, bf16[256,4096]{1,0:T(8,128)(2,1)} %collective-permute-done.14.far, bf16[256,2048]{1,0:T(8,128)(2,1)} %hidden_own.1, bf16[256,2048]{1,0:T(8,128)(2,1)} %collective-permute-done.7.hidden_other, ...), custom_call_target="tpu_custom_call" | custom-call | flops 10000000 | bytes 8000000 | tf_op jit(solution)/shard_map/finish/pallas_call | solution.py:173
  (9 shorter events, 0.1 us)
Async XLA Ops:
  0.6 1.5 %copy-start.3 = (bf16[256,2048]{1,0:T(8,128)(2,1)S(1)}, bf16[256,2048]{1,0:T(8,128)(2,1)}, u32[]{:S(2)}) copy-start(bf16[256,2048]{1,0:T(8,128)(2,1)} %param.9) | copy-start | bytes 3145732
  0.6 1.9 %copy-start.2 = (bf16[256,2048]{1,0:T(8,128)(2,1)S(1)}, bf16[256,2048]{1,0:T(8,128)(2,1)}, u32[]{:S(2)}) copy-start(bf16[256,2048]{1,0:T(8,128)(2,1)} %param.7) | copy-start | bytes 3145732
  3.4 19.2 %copy-start.4 = (s32[2,8]{1,0:T(2,128)S(1)}, s32[2,8]{1,0:T(2,128)}, u32[]{:S(2)}) copy-start(s32[2,8]{1,0:T(2,128)} %param.10) | copy-start | bytes 196
  3.5 12.9 %collective-permute-start.1 = (bf16[512,512]{1,0:T(8,128)(2,1)S(1)}, bf16[512,512]{1,0:T(8,128)(2,1)S(1)}, u32[]{:S(2)}, u32[]{:S(2)}) collective-permute-start(bf16[512,512]{1,0:T(8,128)(2,1)S(1)} %pad_maximum_fusion.3), channel_id=1, source_target_pairs={{0,3},{1,0},{2,1},{3,2},{4,7},{5,4},{6,5},{7,6},{8,11},{9,8},{10,9... | collective-permute-start | bytes 1572872 | tf_op jit(solution)/shard_map/ppermute | solution.py:25
  3.8 13.9 %collective-permute-start = (bf16[512,512]{1,0:T(8,128)(2,1)S(1)}, bf16[512,512]{1,0:T(8,128)(2,1)S(1)}, u32[]{:S(2)}, u32[]{:S(2)}) collective-permute-start(bf16[512,512]{1,0:T(8,128)(2,1)S(1)} %pad_maximum_fusion.1), channel_id=1, source_target_pairs={{0,1},{1,2},{2,3},{3,0},{4,5},{5,6},{6,7},{7,4},{8,9},{9,10},{10,1... | collective-permute-start | bytes 1572872 | tf_op jit(solution)/shard_map/ppermute | solution.py:25
  5.1 30.6 %collective-permute-start.7 = (bf16[256,2048]{1,0:T(8,128)(2,1)}, bf16[256,2048]{1,0:T(8,128)(2,1)}, u32[]{:S(2)}, u32[]{:S(2)}) collective-permute-start(bf16[256,2048]{1,0:T(8,128)(2,1)} %hidden_own.1), channel_id=1, source_target_pairs={{0,128},{128,0},{1,129},{129,1},{2,130},{130,2},{3,131},{131,3},{4... | collective-permute-start | bytes 3145736 | tf_op jit(solution)/shard_map/ppermute | solution.py:33
  17.7 13.6 %collective-permute-start.2 = (bf16[512,512]{1,0:T(8,128)(2,1)}, bf16[512,512]{1,0:T(8,128)(2,1)S(1)}, u32[]{:S(2)}, u32[]{:S(2)}) collective-permute-start(bf16[512,512]{1,0:T(8,128)(2,1)} %pad_maximum_fusion.2), channel_id=1, source_target_pairs={{0,2},{1,3},{2,0},{3,1},{4,6},{5,7},{6,4},{7,5},{8,10},{9,11},{10,... | collective-permute-start | bytes 1572872 | tf_op jit(solution)/shard_map/ppermute | solution.py:25
  19.4 18.4 %collective-permute-start.3 = (bf16[512,512]{1,0:T(8,128)(2,1)S(1)}, bf16[512,512]{1,0:T(8,128)(2,1)S(1)}, u32[]{:S(2)}, u32[]{:S(2)}) collective-permute-start(bf16[512,512]{1,0:T(8,128)(2,1)S(1)} %pad_maximum_fusion.refs_1_), channel_id=1, source_target_pairs={{0,4},{1,5},{2,6},{3,7},{4,8},{5,9},{6,10},{7,11},{8,12},{9,13},{1... | collective-permute-start | bytes 1572872 | tf_op jit(solution)/shard_map/ppermute | solution.py:29
  22.9 24.5 %collective-permute-start.6 = (bf16[512,512]{1,0:T(8,128)(2,1)S(1)}, bf16[512,512]{1,0:T(8,128)(2,1)S(1)}, u32[]{:S(2)}, u32[]{:S(2)}) collective-permute-start(bf16[512,512]{1,0:T(8,128)(2,1)S(1)} %collective-permute-done.1.refs_4_), channel_id=1, source_target_pairs={{0,4},{1,5},{2,6},{3,7},{4,8},{5,9},{6,10},{7,11},{8,12},{9,13},{1... | collective-permute-start | bytes 1572872 | tf_op jit(solution)/shard_map/ppermute | solution.py:29
  26.1 32.6 %collective-permute-start.4 = (bf16[512,512]{1,0:T(8,128)(2,1)S(1)}, bf16[512,512]{1,0:T(8,128)(2,1)S(1)}, u32[]{:S(2)}, u32[]{:S(2)}) collective-permute-start(bf16[512,512]{1,0:T(8,128)(2,1)S(1)} %collective-permute-done.refs_2_), channel_id=1, source_target_pairs={{0,4},{1,5},{2,6},{3,7},{4,8},{5,9},{6,10},{7,11},{8,12},{9,13},{1... | collective-permute-start | bytes 1572872 | tf_op jit(solution)/shard_map/ppermute | solution.py:29
  31.3 38.6 %collective-permute-start.5 = (bf16[512,512]{1,0:T(8,128)(2,1)S(1)}, bf16[512,512]{1,0:T(8,128)(2,1)S(1)}, u32[]{:S(2)}, u32[]{:S(2)}) collective-permute-start(bf16[512,512]{1,0:T(8,128)(2,1)S(1)} %collective-permute-done.2.refs_3_), channel_id=1, source_target_pairs={{0,4},{1,5},{2,6},{3,7},{4,8},{5,9},{6,10},{7,11},{8,12},{9,13},{1... | collective-permute-start | bytes 1572872 | tf_op jit(solution)/shard_map/ppermute | solution.py:29
  35.7 5.8 %collective-permute-start.12 = (bf16[272,512]{1,0:T(8,128)(2,1)S(1)}, bf16[272,512]{1,0:T(8,128)(2,1)S(1)}, u32[]{:S(2)}, u32[]{:S(2)}) collective-permute-start(bf16[272,512]{1,0:T(8,128)(2,1)S(1)} %get-tuple-element.15), channel_id=1, source_target_pairs={{0,3},{1,0},{2,1},{3,2},{4,7},{5,4},{6,5},{7,6},{8,11},{9,8},{10,9... | collective-permute-start | bytes 835592 | tf_op jit(solution)/shard_map/ppermute | solution.py:25
  37.8 41.3 %collective-permute-start.9 = (bf16[272,512]{1,0:T(8,128)(2,1)S(1)}, bf16[272,512]{1,0:T(8,128)(2,1)S(1)}, u32[]{:S(2)}, u32[]{:S(2)}) collective-permute-start(bf16[272,512]{1,0:T(8,128)(2,1)S(1)} %get-tuple-element.12), channel_id=1, source_target_pairs={{0,1},{1,2},{2,3},{3,0},{4,5},{5,6},{6,7},{7,4},{8,9},{9,10},{10,1... | collective-permute-start | bytes 835592 | tf_op jit(solution)/shard_map/ppermute | solution.py:25
  41.5 37.7 %collective-permute-start.8 = (bf16[272,512]{1,0:T(8,128)(2,1)S(1)}, bf16[272,512]{1,0:T(8,128)(2,1)S(1)}, u32[]{:S(2)}, u32[]{:S(2)}) collective-permute-start(bf16[272,512]{1,0:T(8,128)(2,1)S(1)} %get-tuple-element.11), channel_id=1, source_target_pairs={{0,2},{1,3},{2,0},{3,1},{4,6},{5,7},{6,4},{7,5},{8,10},{9,11},{10,... | collective-permute-start | bytes 835592 | tf_op jit(solution)/shard_map/ppermute | solution.py:25
  77.5 11.2 %collective-permute-start.13 = (bf16[256,512]{1,0:T(8,128)(2,1)S(1)}, bf16[256,512]{1,0:T(8,128)(2,1)S(1)}, u32[]{:S(2)}, u32[]{:S(2)}) collective-permute-start(bf16[256,512]{1,0:T(8,128)(2,1)S(1)} %get-tuple-element.16), channel_id=1, source_target_pairs={{0,1},{1,2},{2,3},{3,0},{4,5},{5,6},{6,7},{7,4},{8,9},{9,10},{10,1... | collective-permute-start | bytes 786440 | tf_op jit(solution)/shard_map/ppermute | solution.py:25
  86.8 6.9 %collective-permute-start.10 = (bf16[256,512]{1,0:T(8,128)(2,1)S(1)}, bf16[256,512]{1,0:T(8,128)(2,1)S(1)}, u32[]{:S(2)}, u32[]{:S(2)}) collective-permute-start(bf16[256,512]{1,0:T(8,128)(2,1)S(1)} %get-tuple-element.13), channel_id=1, source_target_pairs={{0,2},{1,3},{2,0},{3,1},{4,6},{5,7},{6,4},{7,5},{8,10},{9,11},{10,... | collective-permute-start | bytes 786440 | tf_op jit(solution)/shard_map/ppermute | solution.py:25
  87.7 12.9 %collective-permute-start.11 = (bf16[256,512]{1,0:T(8,128)(2,1)S(1)}, bf16[256,512]{1,0:T(8,128)(2,1)S(1)}, u32[]{:S(2)}, u32[]{:S(2)}) collective-permute-start(bf16[256,512]{1,0:T(8,128)(2,1)S(1)} %get-tuple-element.14), channel_id=1, source_target_pairs={{0,3},{1,0},{2,1},{3,2},{4,7},{5,4},{6,5},{7,6},{8,11},{9,8},{10,9... | collective-permute-start | bytes 786440 | tf_op jit(solution)/shard_map/ppermute | solution.py:25
  100.6 5.8 %copy-start = (bf16[2048,4096]{1,0:T(8,128)(2,1)S(1)}, bf16[2048,4096]{1,0:T(8,128)(2,1)}, u32[]{:S(2)}) copy-start(bf16[2048,4096]{1,0:T(8,128)(2,1)} %refs_7_.1) | copy-start | bytes 50331652
  106.4 12.7 %copy-start.1 = (f32[2048]{0:T(1024)S(1)}, f32[2048]{0:T(1024)}, u32[]{:S(2)}) copy-start(f32[2048]{0:T(1024)} %param.13) | copy-start | bytes 24580
  113.6 5.5 %collective-permute-start.14 = (bf16[256,4096]{1,0:T(8,128)(2,1)S(1)}, bf16[256,4096]{1,0:T(8,128)(2,1)}, u32[]{:S(2)}, u32[]{:S(2)}) collective-permute-start(bf16[256,4096]{1,0:T(8,128)(2,1)S(1)} %project.1.near), channel_id=1, source_target_pairs={{0,128},{128,0},{1,129},{129,1},{2,130},{130,2},{3,131},{131,3},{4... | collective-permute-start | bytes 6291464 | tf_op jit(solution)/shard_map/ppermute | solution.py:33
